TPU v7x, 128 devices: a whole 4x4x4 slice. The times are simulated.
128 devices in a mesh: lat: 8 (over x, z_lo), lon: 16 (over z_hi, y, core).
Axes of the slice: x: 4, y: 4, z: 4 (z_hi: 2, z_lo: 2; z = z_hi * 2 + z_lo), core: 2. Of those that a mesh axis runs over, the one named last changes fastest.
Arguments:
- gridded_observations: bfloat16 [256, 768, 72], P('lat', 'lon'), may hold values from -6 to 6
- footprint_offsets: int32 [128, 32], replicated, may hold values from 0 to 59, as said below
- coarsening_kernel_entries: bfloat16 [128, 9, 32], replicated, may hold values from -1 to 1
- coarsening_matrix: bfloat16 [648, 512], replicated, may hold values from -0.25 to 0.25
- coarsening_offset: float32 [512], replicated, may hold values from -3 to 3
- first_norm_scale: float32 [512], replicated, may hold values from 0.1 to 1.9
- neighbourhood_kernel_entries: bfloat16 [128, 9, 21], P('lat'), may hold values from -1.25 to 1.25
- polar_kernel_entries: bfloat16 [2, 3, 9, 3, 384], replicated, may hold values from -0.1875 to 0.1875
- mixing_matrix: bfloat16 [4608, 512], replicated, may hold values from -0.09375 to 0.09375
- second_norm_scale: float32 [512], replicated, may hold values from 0.1 to 1.9
- expansion_matrix: bfloat16 [512, 1024], replicated, may hold values from -0.25 to 0.25
- expansion_offset: float32 [1024], replicated, may hold values from -3 to 3
- contraction_matrix: bfloat16 [1024, 512], replicated, may hold values from -0.1875 to 0.1875
Outputs:
- encoded: bfloat16 [128, 384, 512], P('lat', 'lon')
Inputs may be any that keep to these rules, and one draw needn't show every extreme that they name: `footprint_offsets`: in every cycle the 32 entries of support are distinct cells of the 6 x 10 window.
All inputs are finite; a program needn't handle non-finite values.
Results may differ from a plain program's by a relative error of at most 0.018.
Values may be sent and summed in bfloat16 or wider, within the bound.
A program may use at most 128 MiB of HBM per device.

v0:
```python
import functools

import jax
import jax.numpy as jnp
from jax import lax
from jax.experimental import pallas as pl
from jax.experimental.pallas import tpu as pltpu
from jax.sharding import PartitionSpec as P

VARS = 72
FEAT = 512
HIDDEN = 1024
BASIS = 9
RIN = 6
LWIN = 10
CELLS = 32
RLOC = 3
LLOC = 7
CAP = 3
ROWS = 16
COLS = 24
IN_ROWS = 2 * ROWS
IN_COLS = 2 * COLS
EDGE_ROWS = 4
EDGE_COLS = 16
WIDE = EDGE_COLS + IN_COLS + EDGE_COLS
TALL = EDGE_ROWS + IN_ROWS + EDGE_ROWS
EXT_ROWS = ROWS + 2
EXT_COLS = 32
BATCH = 6
SLOT = 4 * COLS
EPS = 1e-05
bf16, f32 = jnp.bfloat16, jnp.float32
MESH = pl.DeviceIdType.MESH

NEAR = [(0, -1), (0, 1), (-1, 0), (1, 0), (-1, -1), (-1, 1), (1, -1), (1, 1)]
FROM_ROWS = {-1: (0, EDGE_ROWS), 0: (0, IN_ROWS), 1: (IN_ROWS - EDGE_ROWS, EDGE_ROWS)}
TO_ROWS = {-1: EDGE_ROWS + IN_ROWS, 0: EDGE_ROWS, 1: 0}
FROM_COLS = {-1: (0, EDGE_COLS), 0: (0, IN_COLS), 1: (IN_COLS - EDGE_COLS, EDGE_COLS)}
TO_COLS = {-1: EDGE_COLS + IN_COLS, 0: EDGE_COLS, 1: 0}


def norm(wide, gain):
    center = jnp.mean(wide, axis=-1, keepdims=True)
    off = wide - center
    spread = jnp.mean(off * off, axis=-1, keepdims=True)
    return off * lax.rsqrt(spread + EPS) * gain


def gelu(u):
    return 0.5 * u * (1.0 + jnp.tanh(0.7978845608 * (u + 0.044715 * (u * u * u))))


def toeplitz(row, count, shift, stride):
    return pltpu.roll(
        jnp.broadcast_to(row, (count, row.shape[1])), shift, 1, stride=stride, stride_axis=0
    )


def kernel(
    nlat, nlon,
    x, foot, cke, cmat, coff, g1, nk, pol, mix, g2, emat, eoff, kmat,
    out,
    xe, footv, ckev, cmv, coffv, g1v, nkv, polv, mixv, g2v, ematv, eoffv, kmatv,
    entv, tapv, polf, poltaps, cmp, w, b, nv, lat, filt, gath, lhs, pres,
    local_sem, near_send, near_recv, cap_send, cap_recv,
):
    la, lo = lax.axis_index("lat"), lax.axis_index("lon")
    north = la == 0
    south = la == nlat - 1
    polar = north | south
    total = nlat * ROWS

    barrier = pltpu.get_barrier_semaphore()

    def there(dy):
        return (la + dy >= 0) & (la + dy < nlat)

    def greet(dy, dx):
        pl.semaphore_signal(
            barrier, inc=1, device_id=(la + dy, lax.rem(lo + dx + nlon, nlon)), device_id_type=MESH
        )

    for dy in (-1, 1):
        @pl.when(there(dy))
        def _():
            for dx in (-1, 0, 1):
                greet(dy, dx)

    @pl.when(jnp.logical_not(polar))
    def _():
        greet(0, -1)
        greet(0, 1)

    @pl.when(polar)
    def _():
        @pl.loop(1, nlon)
        def _(d):
            greet(0, d)

    pairs = [
        (foot, footv),
        (cke, ckev),
        (nk, nkv),
        (x, xe.at[pl.ds(EDGE_ROWS, IN_ROWS), pl.ds(EDGE_COLS, IN_COLS)]),
        (cmat, cmv),
        (coff, coffv),
        (g1, g1v),
        (pol, polv),
        (g2, g2v),
        (eoff, eoffv),
        (mix, mixv),
        (emat, ematv),
        (kmat, kmatv),
    ]
    FOOT, CKE, NK, OWN, CM, COFF, G1, POL, G2, EOFF, MIX, EMAT, KMAT = range(13)
    local = [pltpu.make_async_copy(s, d, local_sem.at[n]) for n, (s, d) in enumerate(pairs)]
    for copy in local:
        copy.start()

    pl.semaphore_wait(
        barrier,
        jnp.where(polar, nlon - 1, 2) + jnp.where(north, 0, 3) + jnp.where(south, 0, 3),
    )

    def near(n):
        dy, dx = NEAR[n]
        r0, rn = FROM_ROWS[dy]
        c0, cn = FROM_COLS[dx]
        return pltpu.make_async_remote_copy(
            src_ref=x.at[pl.ds(r0, rn), pl.ds(c0, cn)],
            dst_ref=xe.at[pl.ds(TO_ROWS[dy], rn), pl.ds(TO_COLS[dx], cn)],
            send_sem=near_send.at[n],
            recv_sem=near_recv.at[n],
            device_id=(la + dy, lax.rem(lo + dx + nlon, nlon)),
            device_id_type=MESH,
        )

    def each_near(act, sign):
        for dy in (0, -1, 1):
            mine = [n for n in range(8) if NEAR[n][0] == dy]

            def go(mine=mine):
                for n in mine:
                    act(near(n))

            if dy == 0:
                go()
            else:
                pl.when(there(sign * dy))(go)

    each_near(lambda c: c.start(), 1)

    @pl.when(north)
    def _():
        xe[0:EDGE_ROWS] = jnp.zeros((EDGE_ROWS, WIDE, VARS), bf16)

    @pl.when(south)
    def _():
        xe[TALL - EDGE_ROWS : TALL] = jnp.zeros((EDGE_ROWS, WIDE, VARS), bf16)

    nv[EXT_ROWS] = jnp.zeros((EXT_COLS, FEAT), bf16)

    for n in (FOOT, CKE, NK):
        local[n].wait()
    chosen = jnp.where(
        lax.broadcasted_iota(jnp.int32, (EXT_COLS, total), 0) + la * ROWS - 1
        == lax.broadcasted_iota(jnp.int32, (EXT_COLS, total), 1),
        1.0,
        0.0,
    ).astype(bf16)
    for k in range(BASIS):
        entries = lax.dot_general(
            chosen, ckev[k], (((1,), (1,)), ((), ())), preferred_element_type=f32
        )
        entv[:, k, :] = entries[:EXT_ROWS]
    cycle = lax.broadcasted_iota(jnp.int32, (CELLS, total), 1)
    place = lax.broadcasted_iota(jnp.int32, (CELLS, 512), 1).astype(f32)

    @pl.loop(0, EXT_ROWS)
    def _(i):
        cells = footv[...]
        lanes = (cells + (WIDE - LWIN) * ((cells * 205) >> 11) + 6).astype(f32)
        column = jnp.sum(
            jnp.where(cycle == la * ROWS + i - 1, lanes, 0.0), axis=1, keepdims=True
        )
        onehot = jnp.where(column == place, 1.0, 0.0).astype(bf16)
        dense = jnp.dot(entv[i].astype(bf16), onehot, preferred_element_type=f32)
        for k in range(BASIS):
            w[i, k * EXT_COLS : (k + 1) * EXT_COLS, :] = toeplitz(
                dense[k : k + 1], EXT_COLS, 0, 2
            ).astype(bf16)

    s = lax.broadcasted_iota(jnp.int32, (RLOC * LLOC, 128), 0)
    lane = lax.broadcasted_iota(jnp.int32, (RLOC * LLOC, 128), 1)
    spread = jnp.where(
        ((lane & 31) < LLOC) & ((lane >> 5) * LLOC + (lane & 31) == s), 1.0, 0.0
    ).astype(bf16)
    for k in range(BASIS):
        tapv[k] = jnp.dot(nkv[k], spread, preferred_element_type=f32)

    @pl.loop(0, ROWS)
    def _(i):
        b[i] = jnp.concatenate(
            [toeplitz(tapv[k, pl.ds(i, 1), :], COLS, 0, 1) for k in range(BASIS)], axis=0
        ).astype(bf16)

    local[CM].wait()
    for k in range(BASIS):
        cmp[k * 128 : k * 128 + VARS, :] = cmv[k * VARS : (k + 1) * VARS, :]
        cmp[k * 128 + VARS : (k + 1) * 128, :] = jnp.zeros((128 - VARS, FEAT), bf16)

    for n in (COFF, G1, OWN):
        local[n].wait()
    each_near(lambda c: c.wait_recv(), -1)

    first = jnp.where(la < nlat // 2, 1, ROWS - 3)
    offset = coffv[...].reshape(1, FEAT)
    gain = g1v[...].reshape(1, FEAT)

    def cap(d):
        return pltpu.make_async_remote_copy(
            src_ref=gath.at[0],
            dst_ref=gath.at[nlon - d],
            send_sem=cap_send.at[d - 1],
            recv_sem=cap_recv.at[d - 1],
            device_id=(la, lax.rem(lo + d, nlon)),
            device_id_type=MESH,
        )

    @pl.loop(0, EXT_ROWS // BATCH)
    def _(batch):
        parts = []
        for m in range(BATCH):
            i = lax.rem(first + batch * BATCH + m, EXT_ROWS)
            window = xe[pl.ds(2 * i, RIN)].reshape(RIN * WIDE, VARS)
            window = jnp.concatenate(
                [window, jnp.zeros((RIN * WIDE, 128 - VARS), bf16)], axis=1
            )
            window = jnp.concatenate([window, jnp.zeros((512 - RIN * WIDE, 128), bf16)], axis=0)
            got = jnp.dot(w[i], window, preferred_element_type=f32).astype(bf16)
            parts.append(
                jnp.concatenate(
                    [got[k * EXT_COLS : (k + 1) * EXT_COLS] for k in range(BASIS)], axis=1
                )
            )
        latent = jnp.dot(
            jnp.concatenate(parts, axis=0), cmp[...], preferred_element_type=f32
        )
        latent = (latent + offset).astype(bf16).astype(f32)
        normed = norm(latent, gain)
        for m in range(BATCH):
            i = lax.rem(first + batch * BATCH + m, EXT_ROWS)
            g = la * ROWS + i - 1
            lat[i] = latent[m * EXT_COLS : (m + 1) * EXT_COLS]
            row = normed[m * EXT_COLS : (m + 1) * EXT_COLS]
            nv[i] = jnp.where((g >= 0) & (g < total), row, 0.0).astype(bf16)

        @pl.when(polar & (batch == 0))
        def _():
            rows = [
                normed[m * EXT_COLS + 3 : m * EXT_COLS + 3 + COLS] for m in range(4)
            ]
            gath[0] = jnp.concatenate(rows, axis=0).astype(bf16)

            @pl.loop(1, nlon)
            def _(d):
                cap(d).start()

    span = nlon * SLOT

    @pl.when(polar)
    def _():
        local[POL].wait()
        lon_of = lax.broadcasted_iota(jnp.int32, (nlon * COLS, span), 0)
        at = lax.broadcasted_iota(jnp.int32, (nlon * COLS, span), 1)
        dev = at // SLOT
        pick = jnp.where(
            (at - dev * SLOT < COLS) & (dev * COLS + (at - dev * SLOT) == lon_of), 1.0, 0.0
        ).astype(bf16)
        at = lax.broadcasted_iota(jnp.int32, (COLS, span), 1)
        row = lax.broadcasted_iota(jnp.int32, (COLS, span), 0)
        inside = lax.rem(at, COLS) >= row
        cycle = lax.rem(lax.broadcasted_iota(jnp.int32, (1, span), 1), SLOT) // COLS
        lead = jnp.where(north, 1, 0)
        for t in range(CAP):
            for k in range(BASIS):
                for r in range(RLOC):
                    both = polv[t, k, r].astype(f32)
                    n = (t * BASIS + k) * RLOC + r
                    polf[n : n + 1, :] = jnp.where(north, both[0:1], both[1:2])
        poltaps[...] = jnp.dot(polf[...].astype(bf16), pick, preferred_element_type=f32)
        for t in range(CAP):

            @pl.loop(0, BASIS)
            def _(k):
                line = jnp.zeros((1, span), f32)
                for r in range(RLOC):
                    tap = poltaps[pl.ds((t * BASIS + k) * RLOC + r, 1), :]
                    moved = jnp.where(
                        north,
                        pltpu.roll(tap, (COLS * (t + r - 1)) % span, 1),
                        pltpu.roll(tap, COLS * (t + r), 1),
                    )
                    line = line + jnp.where(cycle == t + r - lead, moved, 0.0)
                lhs[t, pl.ds(k * COLS, COLS), :] = jnp.where(
                    inside, toeplitz(line, COLS, 0, 1), toeplitz(line, COLS, SLOT - COLS, 1)
                )

    def filters(i, extra):
        rhs = nv[pl.ds(i, 4)].reshape(4 * EXT_COLS, FEAT)
        got = jnp.dot(b[i], rhs, preferred_element_type=f32)
        return got if extra is None else got + extra

    def filter_pair(i, extra):
        one = filters(i, None if extra is None else pres[extra])
        two = filters(i + 1, None if extra is None else pres[extra + 1])
        for k in range(BASIS):
            both = jnp.concatenate(
                [one[k * COLS : (k + 1) * COLS], two[k * COLS : (k + 1) * COLS]], axis=0
            )
            filt[
                pl.ds(pl.multiple_of(i * COLS, 2 * COLS), 2 * COLS), k * FEAT : (k + 1) * FEAT
            ] = both.astype(bf16)

    expand_offset = eoffv
    gain_two = g2v

    def finish(i, rows):
        at = pl.ds(pl.multiple_of(i * COLS, 4 * COLS), rows * COLS)
        residual = lat[pl.ds(i + 1, rows), 3 : 3 + COLS, :].reshape(rows * COLS, FEAT)
        middle = residual + jnp.dot(filt[at, :], mixv[...], preferred_element_type=f32)
        middle = middle.astype(bf16).astype(f32)
        normed = norm(middle, gain_two[...].reshape(1, FEAT)).astype(bf16)
        hidden = jnp.dot(normed, ematv[...], preferred_element_type=f32)
        hidden = gelu(hidden + expand_offset[...].reshape(1, HIDDEN)).astype(bf16)
        encoded = middle + jnp.dot(hidden, kmatv[...], preferred_element_type=f32)
        out[at, :] = encoded.astype(bf16)

    upper = la < nlat // 2
    big, small = jnp.where(upper, 4, 0), jnp.where(upper, 0, ROWS - 4)

    @pl.loop(0, (ROWS - 4) // 2)
    def _(n):
        filter_pair(big + 2 * n, None)

    for n in (G2, EOFF, MIX, EMAT, KMAT):
        local[n].wait()
    finish(big, ROWS - 4)

    pres[...] = jnp.zeros(pres.shape, f32)

    @pl.when(polar)
    def _():
        @pl.loop(1, nlon)
        def _(d):
            cap(d).wait_recv()

        lead = jnp.where(north, 0, 1)
        everything = gath[...].reshape(span, FEAT)
        for t in range(CAP):
            pres[t + lead] = jnp.dot(
                lhs[t].astype(bf16), everything, preferred_element_type=f32
            )

    filter_pair(small, 0)
    filter_pair(small + 2, 2)
    finish(small, 4)

    each_near(lambda c: c.wait_send(), 1)

    @pl.when(polar)
    def _():
        @pl.loop(1, nlon)
        def _(d):
            cap(d).wait_send()

    @pl.when(jnp.logical_not(polar))
    def _():
        local[POL].wait()


def body(x, foot, cke, cmat, coff, g1, nk, pol, mix, g2, emat, eoff, kmat):
    nlat, nlon = lax.axis_size("lat"), lax.axis_size("lon")
    span = nlon * SLOT
    vmem = pltpu.VMEM
    scratch = [
        vmem((TALL, WIDE, VARS), bf16),
        vmem((CELLS, nlat * ROWS), jnp.int32),
        vmem((BASIS, CELLS, nlat * ROWS), bf16),
        vmem((BASIS * VARS, FEAT), bf16),
        vmem((FEAT,), f32),
        vmem((FEAT,), f32),
        vmem((BASIS, ROWS, RLOC * LLOC), bf16),
        vmem((CAP, BASIS, RLOC, 2, nlon * COLS), bf16),
        vmem((BASIS * FEAT, FEAT), bf16),
        vmem((FEAT,), f32),
        vmem((FEAT, HIDDEN), bf16),
        vmem((HIDDEN,), f32),
        vmem((HIDDEN, FEAT), bf16),
        vmem((EXT_ROWS, BASIS, CELLS), f32),
        vmem((BASIS, ROWS, 128), f32),
        vmem((CAP * BASIS * RLOC, nlon * COLS), f32),
        vmem((CAP * BASIS * RLOC, span), f32),
        vmem((BASIS * 128, FEAT), bf16),
        vmem((EXT_ROWS, BASIS * EXT_COLS, 512), bf16),
        vmem((ROWS, BASIS * COLS, 128), bf16),
        vmem((EXT_ROWS + 1, EXT_COLS, FEAT), bf16),
        vmem((EXT_ROWS, EXT_COLS, FEAT), f32),
        vmem((ROWS * COLS, BASIS * FEAT), bf16),
        vmem((nlon, SLOT, FEAT), bf16),
        vmem((CAP, BASIS * COLS, span), f32),
        vmem((4, BASIS * COLS, FEAT), f32),
        pltpu.SemaphoreType.DMA((13,)),
        pltpu.SemaphoreType.DMA((8,)),
        pltpu.SemaphoreType.DMA((8,)),
        pltpu.SemaphoreType.DMA((nlon - 1,)),
        pltpu.SemaphoreType.DMA((nlon - 1,)),
    ]
    encoded = pl.pallas_call(
        functools.partial(kernel, nlat, nlon),
        out_shape=jax.ShapeDtypeStruct((ROWS * COLS, FEAT), bf16),
        in_specs=[pl.BlockSpec(memory_space=pl.ANY)] * 13,
        out_specs=pl.BlockSpec(memory_space=pltpu.VMEM),
        scratch_shapes=scratch,
        compiler_params=pltpu.CompilerParams(
            collective_id=0, has_side_effects=True, vmem_limit_bytes=56 << 20
        ),
        cost_estimate=pl.CostEstimate(
            flops=3_000_000_000, bytes_accessed=9_000_000, transcendentals=400_000
        ),
    )(
        x,
        foot.T,
        cke.transpose(1, 2, 0),
        cmat,
        coff,
        g1,
        nk.transpose(1, 0, 2),
        pol.transpose(1, 2, 3, 0, 4),
        mix,
        g2,
        emat,
        eoff,
        kmat,
    )
    return encoded.reshape(ROWS, COLS, FEAT)


def solution(mesh):
    return jax.shard_map(
        body,
        mesh=mesh,
        in_specs=(
            P("lat", "lon", None),
            P(),
            P(),
            P(),
            P(),
            P(),
            P("lat", None, None),
            P(),
            P(),
            P(),
            P(),
            P(),
            P(),
        ),
        out_specs=P("lat", "lon", None),
        check_vma=False,
    )
```

profile of v0, /device:TPU:1, one launch (start us, length us, event | category | flops | bytes accessed | tf_op | source)
XLA Modules:
  0.0 46.7 jit_solution(10165606383406686205)
XLA Ops:
  0.0 44.9 %shard_map.127 = bf16[384,512]{1,0:T(8,128)(2,1)} custom-call(bf16[32,48,72]{2,1,0:T(8,128)(2,1)} %x.1, s32[32,128]{1,0:T(8,128)} %bitcast.9, bf16[9,32,128]{2,1,0:T(8,128)(2,1)} %bitcast.7, bf16[648,512]{1,0:T(8,128)(2,1)} %cmat.1, f32[512]{0:T(512)} %coff.1, f32[512]{0:T(512)} %g1.1, bf16[9,16,21]{2,1,0:T(8,128)(2,1)} %bitcast.8, ...), custom_call_target="tpu_custom_call" | custom-call | flops 3000000000 | bytes 9000000 | tf_op jit(solution)/shard_map/pallas_call | solution.py:420
  44.9 1.8 %copy.15 = bf16[16,24,512]{2,1,0:T(8,128)(2,1)} copy(bf16[16,24,512]{2,1,0:T(8,128)(2,1)} %bitcast.5) | data formatting | bytes 786432
where the time goes:
time: 46.8 us; the launch traced here: 46.7 us
  Pallas kernels  44.9 us (96%)
  local copies, waits for them, and re-layouts  1.77 us (4%)
    pallas_call x1, Pallas kernels, body(): pl.pallas_call(functools.partial(kernel, nlat, nlon), out_shape=jax.Shape...  44.9 us
    unnamed x1, local copies, waits for them, and re-layouts  1.77 us

commit v1 on v0

--- a/solution.py
+++ b/solution.py
@@ -27,17 +27,19 @@
 TALL = EDGE_ROWS + IN_ROWS + EDGE_ROWS
 EXT_ROWS = ROWS + 2
 EXT_COLS = 32
-BATCH = 6
 SLOT = 4 * COLS
 EPS = 1e-05
 bf16, f32 = jnp.bfloat16, jnp.float32
 MESH = pl.DeviceIdType.MESH
 
-NEAR = [(0, -1), (0, 1), (-1, 0), (1, 0), (-1, -1), (-1, 1), (1, -1), (1, 1)]
-FROM_ROWS = {-1: (0, EDGE_ROWS), 0: (0, IN_ROWS), 1: (IN_ROWS - EDGE_ROWS, EDGE_ROWS)}
-TO_ROWS = {-1: EDGE_ROWS + IN_ROWS, 0: EDGE_ROWS, 1: 0}
+HALF = IN_ROWS // 2
+NEAR = [(0, -1), (0, 1), (0, -1), (0, 1)] + [(dy, dx) for dy in (-1, 1) for dx in (-1, 0, 1)]
+FROM_ROWS = {-1: 0, 1: IN_ROWS - EDGE_ROWS}
+TO_ROWS = {-1: EDGE_ROWS + IN_ROWS, 1: 0}
 FROM_COLS = {-1: (0, EDGE_COLS), 0: (0, IN_COLS), 1: (IN_COLS - EDGE_COLS, EDGE_COLS)}
 TO_COLS = {-1: EDGE_COLS + IN_COLS, 0: EDGE_COLS, 1: 0}
+GROUP = 8
+WINDOW = 32
 
 
 def norm(wide, gain):
@@ -62,14 +64,18 @@
     x, foot, cke, cmat, coff, g1, nk, pol, mix, g2, emat, eoff, kmat,
     out,
     xe, footv, ckev, cmv, coffv, g1v, nkv, polv, mixv, g2v, ematv, eoffv, kmatv,
-    entv, tapv, polf, poltaps, cmp, w, b, nv, lat, filt, gath, lhs, pres,
-    local_sem, near_send, near_recv, cap_send, cap_recv,
+    entv, tapv, polf, poltaps, lines, cmp, w, b, nv, lat, filt, gath, lhs, pres,
+    local_sem, near_send, near_recv, cap_send, cap_recv, hand_send, hand_recv,
 ):
     la, lo = lax.axis_index("lat"), lax.axis_index("lon")
     north = la == 0
     south = la == nlat - 1
     polar = north | south
+    upper = la < nlat // 2
     total = nlat * ROWS
+    chips = nlon // 2
+    core = lax.rem(lo, 2)
+    sibling = lo + 1 - 2 * core
 
     barrier = pltpu.get_barrier_semaphore()
 
@@ -87,16 +93,13 @@
             for dx in (-1, 0, 1):
                 greet(dy, dx)
 
-    @pl.when(jnp.logical_not(polar))
-    def _():
-        greet(0, -1)
-        greet(0, 1)
+    greet(0, -1)
+    greet(0, 1)
 
     @pl.when(polar)
     def _():
-        @pl.loop(1, nlon)
-        def _(d):
-            greet(0, d)
+        for m in range(1, chips):
+            greet(0, 2 * m)
 
     pairs = [
         (foot, footv),
@@ -115,41 +118,49 @@
     ]
     FOOT, CKE, NK, OWN, CM, COFF, G1, POL, G2, EOFF, MIX, EMAT, KMAT = range(13)
     local = [pltpu.make_async_copy(s, d, local_sem.at[n]) for n, (s, d) in enumerate(pairs)]
-    for copy in local:
-        copy.start()
+    for n in (FOOT, CKE, NK, OWN):
+        local[n].start()
 
     pl.semaphore_wait(
         barrier,
-        jnp.where(polar, nlon - 1, 2) + jnp.where(north, 0, 3) + jnp.where(south, 0, 3),
+        2 + jnp.where(polar, chips - 1, 0) + jnp.where(north, 0, 3) + jnp.where(south, 0, 3),
     )
 
     def near(n):
         dy, dx = NEAR[n]
-        r0, rn = FROM_ROWS[dy]
         c0, cn = FROM_COLS[dx]
+        if n < 2:
+            r0, rn = jnp.where(upper, 0, HALF), HALF
+            to = r0 + EDGE_ROWS
+        elif n < 4:
+            r0, rn = jnp.where(upper, HALF, 0), HALF
+            to = r0 + EDGE_ROWS
+        else:
+            r0, rn, to = FROM_ROWS[dy], EDGE_ROWS, TO_ROWS[dy]
         return pltpu.make_async_remote_copy(
             src_ref=x.at[pl.ds(r0, rn), pl.ds(c0, cn)],
-            dst_ref=xe.at[pl.ds(TO_ROWS[dy], rn), pl.ds(TO_COLS[dx], cn)],
+            dst_ref=xe.at[pl.ds(to, rn), pl.ds(TO_COLS[dx], cn)],
             send_sem=near_send.at[n],
             recv_sem=near_recv.at[n],
             device_id=(la + dy, lax.rem(lo + dx + nlon, nlon)),
             device_id_type=MESH,
         )
 
-    def each_near(act, sign):
-        for dy in (0, -1, 1):
-            mine = [n for n in range(8) if NEAR[n][0] == dy]
-
-            def go(mine=mine):
-                for n in mine:
-                    act(near(n))
-
-            if dy == 0:
-                go()
-            else:
-                pl.when(there(sign * dy))(go)
-
-    each_near(lambda c: c.start(), 1)
+    def each_near(act, sign, first, last):
+        for n in range(first, min(last, 4)):
+            act(near(n))
+        if last > 4:
+            for dy in (-1, 1):
+
+                @pl.when(there(sign * dy))
+                def _():
+                    for n in range(4, 10):
+                        if NEAR[n][0] == dy:
+                            act(near(n))
+
+    each_near(lambda c: c.start(), 1, 0, 10)
+    for n in (CM, COFF, G1, POL, G2, EOFF, MIX, EMAT, KMAT):
+        local[n].start()
 
     @pl.when(north)
     def _():
@@ -175,21 +186,20 @@
         )
         entv[:, k, :] = entries[:EXT_ROWS]
     cycle = lax.broadcasted_iota(jnp.int32, (CELLS, total), 1)
-    place = lax.broadcasted_iota(jnp.int32, (CELLS, 512), 1).astype(f32)
+    place = lax.broadcasted_iota(jnp.int32, (CELLS, 256), 1).astype(f32)
 
     @pl.loop(0, EXT_ROWS)
     def _(i):
         cells = footv[...]
-        lanes = (cells + (WIDE - LWIN) * ((cells * 205) >> 11) + 6).astype(f32)
+        lanes = (cells + (WINDOW - LWIN) * ((cells * 205) >> 11) + 6).astype(f32)
         column = jnp.sum(
             jnp.where(cycle == la * ROWS + i - 1, lanes, 0.0), axis=1, keepdims=True
         )
         onehot = jnp.where(column == place, 1.0, 0.0).astype(bf16)
         dense = jnp.dot(entv[i].astype(bf16), onehot, preferred_element_type=f32)
-        for k in range(BASIS):
-            w[i, k * EXT_COLS : (k + 1) * EXT_COLS, :] = toeplitz(
-                dense[k : k + 1], EXT_COLS, 0, 2
-            ).astype(bf16)
+        w[i] = jnp.concatenate(
+            [toeplitz(dense[k : k + 1], GROUP, 0, 2) for k in range(BASIS)], axis=0
+        ).astype(bf16)
 
     s = lax.broadcasted_iota(jnp.int32, (RLOC * LLOC, 128), 0)
     lane = lax.broadcasted_iota(jnp.int32, (RLOC * LLOC, 128), 1)
@@ -212,100 +222,155 @@
 
     for n in (COFF, G1, OWN):
         local[n].wait()
-    each_near(lambda c: c.wait_recv(), -1)
-
-    first = jnp.where(la < nlat // 2, 1, ROWS - 3)
+
+    first = jnp.where(upper, 1, ROWS - 3)
     offset = coffv[...].reshape(1, FEAT)
     gain = g1v[...].reshape(1, FEAT)
 
-    def cap(d):
-        return pltpu.make_async_remote_copy(
-            src_ref=gath.at[0],
-            dst_ref=gath.at[nlon - d],
-            send_sem=cap_send.at[d - 1],
-            recv_sem=cap_recv.at[d - 1],
-            device_id=(la, lax.rem(lo + d, nlon)),
-            device_id_type=MESH,
-        )
-
-    @pl.loop(0, EXT_ROWS // BATCH)
-    def _(batch):
+    def coarsen(begin, count):
         parts = []
-        for m in range(BATCH):
-            i = lax.rem(first + batch * BATCH + m, EXT_ROWS)
-            window = xe[pl.ds(2 * i, RIN)].reshape(RIN * WIDE, VARS)
-            window = jnp.concatenate(
-                [window, jnp.zeros((RIN * WIDE, 128 - VARS), bf16)], axis=1
+        for m in range(count):
+            i = lax.rem(begin + m, EXT_ROWS)
+            rows = xe[pl.ds(2 * i, RIN)]
+            windows = [
+                jnp.concatenate(
+                    [
+                        rows[:, 16 * a : 16 * a + WINDOW, :].reshape(RIN * WINDOW, VARS),
+                        jnp.zeros((RIN * WINDOW, 128 - VARS), bf16),
+                    ],
+                    axis=1,
+                )
+                for a in range(EXT_COLS // GROUP)
+            ]
+            windows = jnp.concatenate(windows, axis=1)
+            windows = jnp.concatenate(
+                [windows, jnp.zeros((256 - RIN * WINDOW, windows.shape[1]), bf16)], axis=0
             )
-            window = jnp.concatenate([window, jnp.zeros((512 - RIN * WIDE, 128), bf16)], axis=0)
-            got = jnp.dot(w[i], window, preferred_element_type=f32).astype(bf16)
-            parts.append(
-                jnp.concatenate(
-                    [got[k * EXT_COLS : (k + 1) * EXT_COLS] for k in range(BASIS)], axis=1
+            got = jnp.dot(w[i], windows, preferred_element_type=f32)
+            for a in range(EXT_COLS // GROUP):
+                parts.append(
+                    jnp.concatenate(
+                        [
+                            got[k * GROUP : (k + 1) * GROUP, a * 128 : (a + 1) * 128]
+                            for k in range(BASIS)
+                        ],
+                        axis=1,
+                    )
                 )
-            )
         latent = jnp.dot(
-            jnp.concatenate(parts, axis=0), cmp[...], preferred_element_type=f32
+            jnp.concatenate(parts, axis=0).astype(bf16), cmp[...], preferred_element_type=f32
         )
         latent = (latent + offset).astype(bf16).astype(f32)
         normed = norm(latent, gain)
-        for m in range(BATCH):
-            i = lax.rem(first + batch * BATCH + m, EXT_ROWS)
+        for m in range(count):
+            i = lax.rem(begin + m, EXT_ROWS)
             g = la * ROWS + i - 1
             lat[i] = latent[m * EXT_COLS : (m + 1) * EXT_COLS]
             row = normed[m * EXT_COLS : (m + 1) * EXT_COLS]
             nv[i] = jnp.where((g >= 0) & (g < total), row, 0.0).astype(bf16)
-
-        @pl.when(polar & (batch == 0))
+        return normed
+
+    def cap(m):
+        return pltpu.make_async_remote_copy(
+            src_ref=gath.at[0],
+            dst_ref=gath.at[nlon - 2 * m],
+            send_sem=cap_send.at[m - 1],
+            recv_sem=cap_recv.at[m - 1],
+            device_id=(la, lax.rem(lo + 2 * m, nlon)),
+            device_id_type=MESH,
+        )
+
+    def hand(m, out=True):
+        slot = (nlon - 2 * m) % nlon
+        west = jnp.where(core == 0, nlon - 1, 1) if out else jnp.where(core == 0, 1, nlon - 1)
+        return pltpu.make_async_remote_copy(
+            src_ref=gath.at[slot],
+            dst_ref=gath.at[lax.rem(slot + west, nlon)],
+            send_sem=hand_send.at[m],
+            recv_sem=hand_recv.at[m],
+            device_id=(la, sibling),
+            device_id_type=MESH,
+        )
+
+    def pass_on(ms):
+        @pl.when(polar)
         def _():
-            rows = [
-                normed[m * EXT_COLS + 3 : m * EXT_COLS + 3 + COLS] for m in range(4)
-            ]
-            gath[0] = jnp.concatenate(rows, axis=0).astype(bf16)
-
-            @pl.loop(1, nlon)
-            def _(d):
-                cap(d).start()
+            for m in ms:
+                cap(m).wait_recv()
+                hand(m).start()
+
+    each_near(lambda c: c.wait_recv(), -1, 0, 2)
+
+    @pl.when(jnp.logical_not(polar))
+    def _():
+        each_near(lambda c: c.wait_recv(), -1, 2, 10)
+
+    normed = coarsen(first, 4)
+
+    @pl.when(polar)
+    def _():
+        rows = [normed[m * EXT_COLS + 3 : m * EXT_COLS + 3 + COLS] for m in range(4)]
+        gath[0] = jnp.concatenate(rows, axis=0).astype(bf16)
+        for m in range(1, chips):
+            cap(m).start()
+        hand(0).start()
+        each_near(lambda c: c.wait_recv(), -1, 2, 10)
+
+    order = sorted(range(1, chips), key=lambda m: (min(m, chips - m), m))
+    third = -(-len(order) // 3)
+
+    @pl.loop(0, 2)
+    def _(n):
+        coarsen(first + 4 + 7 * n, 7)
 
     span = nlon * SLOT
 
     @pl.when(polar)
     def _():
         local[POL].wait()
-        lon_of = lax.broadcasted_iota(jnp.int32, (nlon * COLS, span), 0)
-        at = lax.broadcasted_iota(jnp.int32, (nlon * COLS, span), 1)
-        dev = at // SLOT
+        lane = lax.broadcasted_iota(jnp.int32, (1, span), 1)
+        dev = lane // SLOT
+        inner = lane - dev * SLOT
+        cycle = inner // COLS
+        inner = inner - cycle * COLS
+        source = jnp.where(cycle == 0, dev * COLS + inner, -1)
         pick = jnp.where(
-            (at - dev * SLOT < COLS) & (dev * COLS + (at - dev * SLOT) == lon_of), 1.0, 0.0
+            lax.broadcasted_iota(jnp.int32, (nlon * COLS, span), 0) == source, 1.0, 0.0
         ).astype(bf16)
-        at = lax.broadcasted_iota(jnp.int32, (COLS, span), 1)
-        row = lax.broadcasted_iota(jnp.int32, (COLS, span), 0)
-        inside = lax.rem(at, COLS) >= row
-        cycle = lax.rem(lax.broadcasted_iota(jnp.int32, (1, span), 1), SLOT) // COLS
         lead = jnp.where(north, 1, 0)
+        polf[...] = jnp.zeros(polf.shape, f32)
         for t in range(CAP):
-            for k in range(BASIS):
-                for r in range(RLOC):
+            for r in range(RLOC):
+                for k in range(BASIS):
                     both = polv[t, k, r].astype(f32)
-                    n = (t * BASIS + k) * RLOC + r
+                    n = (t * RLOC + r) * 16 + k
                     polf[n : n + 1, :] = jnp.where(north, both[0:1], both[1:2])
         poltaps[...] = jnp.dot(polf[...].astype(bf16), pick, preferred_element_type=f32)
         for t in range(CAP):
-
-            @pl.loop(0, BASIS)
-            def _(k):
-                line = jnp.zeros((1, span), f32)
-                for r in range(RLOC):
-                    tap = poltaps[pl.ds((t * BASIS + k) * RLOC + r, 1), :]
-                    moved = jnp.where(
-                        north,
-                        pltpu.roll(tap, (COLS * (t + r - 1)) % span, 1),
-                        pltpu.roll(tap, COLS * (t + r), 1),
-                    )
-                    line = line + jnp.where(cycle == t + r - lead, moved, 0.0)
-                lhs[t, pl.ds(k * COLS, COLS), :] = jnp.where(
-                    inside, toeplitz(line, COLS, 0, 1), toeplitz(line, COLS, SLOT - COLS, 1)
-                )
+            line = jnp.zeros((16, span), f32)
+            for r in range(RLOC):
+                n = (t * RLOC + r) * 16
+                to = t + r - lead
+                moved = pltpu.roll(poltaps[n : n + 16, :], lax.rem(COLS * to + span, span), 1)
+                line = line + jnp.where(cycle == to, moved, 0.0)
+            lines[t * 16 : (t + 1) * 16, :] = line
+        inside = inner >= lax.broadcasted_iota(jnp.int32, (COLS, span), 0)
+
+        def circulant(n):
+            t = n // BASIS
+            line = lines[pl.ds(t * 16 + n - t * BASIS, 1), :]
+            return jnp.where(
+                inside, toeplitz(line, COLS, 0, 1), toeplitz(line, COLS, SLOT - COLS, 1)
+            )
+
+        @pl.loop(0, (CAP * BASIS + 1) // 2)
+        def _(n):
+            both = jnp.concatenate(
+                [circulant(2 * n), circulant(jnp.minimum(2 * n + 1, CAP * BASIS - 1))], axis=0
+            )
+            lhs[pl.ds(pl.multiple_of(2 * COLS * n, 2 * COLS), 2 * COLS), :] = both.astype(bf16)
+
+    pass_on(order[:third])
 
     def filters(i, extra):
         rhs = nv[pl.ds(i, 4)].reshape(4 * EXT_COLS, FEAT)
@@ -337,43 +402,41 @@
         encoded = middle + jnp.dot(hidden, kmatv[...], preferred_element_type=f32)
         out[at, :] = encoded.astype(bf16)
 
-    upper = la < nlat // 2
     big, small = jnp.where(upper, 4, 0), jnp.where(upper, 0, ROWS - 4)
 
     @pl.loop(0, (ROWS - 4) // 2)
     def _(n):
         filter_pair(big + 2 * n, None)
 
+    pass_on(order[third : 2 * third])
     for n in (G2, EOFF, MIX, EMAT, KMAT):
         local[n].wait()
     finish(big, ROWS - 4)
+    pass_on(order[2 * third :])
 
     pres[...] = jnp.zeros(pres.shape, f32)
 
     @pl.when(polar)
     def _():
-        @pl.loop(1, nlon)
-        def _(d):
-            cap(d).wait_recv()
-
+        for m in range(chips):
+            hand(m, False).wait_recv()
         lead = jnp.where(north, 0, 1)
-        everything = gath[...].reshape(span, FEAT)
+        got = jnp.dot(lhs[...], gath[...].reshape(span, FEAT), preferred_element_type=f32)
         for t in range(CAP):
-            pres[t + lead] = jnp.dot(
-                lhs[t].astype(bf16), everything, preferred_element_type=f32
-            )
+            pres[t + lead] = got[t * BASIS * COLS : (t + 1) * BASIS * COLS]
 
     filter_pair(small, 0)
     filter_pair(small + 2, 2)
     finish(small, 4)
 
-    each_near(lambda c: c.wait_send(), 1)
+    each_near(lambda c: c.wait_send(), 1, 0, 10)
 
     @pl.when(polar)
     def _():
-        @pl.loop(1, nlon)
-        def _(d):
-            cap(d).wait_send()
+        for m in range(1, chips):
+            cap(m).wait_send()
+        for m in range(chips):
+            hand(m).wait_send()
 
     @pl.when(jnp.logical_not(polar))
     def _():
@@ -400,22 +463,25 @@
         vmem((HIDDEN, FEAT), bf16),
         vmem((EXT_ROWS, BASIS, CELLS), f32),
         vmem((BASIS, ROWS, 128), f32),
-        vmem((CAP * BASIS * RLOC, nlon * COLS), f32),
-        vmem((CAP * BASIS * RLOC, span), f32),
+        vmem((CAP * RLOC * 16, nlon * COLS), f32),
+        vmem((CAP * RLOC * 16, span), f32),
+        vmem((CAP * 16, span), f32),
         vmem((BASIS * 128, FEAT), bf16),
-        vmem((EXT_ROWS, BASIS * EXT_COLS, 512), bf16),
+        vmem((EXT_ROWS, BASIS * GROUP, 256), bf16),
         vmem((ROWS, BASIS * COLS, 128), bf16),
         vmem((EXT_ROWS + 1, EXT_COLS, FEAT), bf16),
         vmem((EXT_ROWS, EXT_COLS, FEAT), f32),
         vmem((ROWS * COLS, BASIS * FEAT), bf16),
         vmem((nlon, SLOT, FEAT), bf16),
-        vmem((CAP, BASIS * COLS, span), f32),
+        vmem(((CAP * BASIS + 1) * COLS, span), bf16),
         vmem((4, BASIS * COLS, FEAT), f32),
         pltpu.SemaphoreType.DMA((13,)),
-        pltpu.SemaphoreType.DMA((8,)),
-        pltpu.SemaphoreType.DMA((8,)),
-        pltpu.SemaphoreType.DMA((nlon - 1,)),
-        pltpu.SemaphoreType.DMA((nlon - 1,)),
+        pltpu.SemaphoreType.DMA((10,)),
+        pltpu.SemaphoreType.DMA((10,)),
+        pltpu.SemaphoreType.DMA((nlon // 2 - 1,)),
+        pltpu.SemaphoreType.DMA((nlon // 2 - 1,)),
+        pltpu.SemaphoreType.DMA((nlon // 2,)),
+        pltpu.SemaphoreType.DMA((nlon // 2,)),
     ]
     encoded = pl.pallas_call(
         functools.partial(kernel, nlat, nlon),

time: 46.8 us -> 36.8 us (0.79)
  Pallas kernels: 44.9 us -> 34.7 us
    pallas_call x1, Pallas kernels: 44.9 us -> 34.7 us  [body(): pl.pallas_call(functools.partial(kernel, nlat, nlon), out_shape=jax.Shape...]
where the time goes in v1:
time: 36.8 us; the launch traced here: 36.5 us
  Pallas kernels  34.7 us (94%)
  local copies, waits for them, and re-layouts  1.77 us (5%)
    pallas_call x1, Pallas kernels, body(): pl.pallas_call(functools.partial(kernel, nlat, nlon), out_shape=jax.Shape...  34.7 us
    unnamed x1, local copies, waits for them, and re-layouts  1.77 us

profile of v1, /device:TPU:1, one launch (start us, length us, event | category | flops | bytes accessed | tf_op | source)
XLA Modules:
  0.0 36.5 jit_solution(12194700932789695976)
XLA Ops:
  0.0 34.7 %shard_map.127 = bf16[384,512]{1,0:T(8,128)(2,1)} custom-call(bf16[32,48,72]{2,1,0:T(8,128)(2,1)} %x.1, s32[32,128]{1,0:T(8,128)} %bitcast.9, bf16[9,32,128]{2,1,0:T(8,128)(2,1)} %bitcast.7, bf16[648,512]{1,0:T(8,128)(2,1)} %cmat.1, f32[512]{0:T(512)} %coff.1, f32[512]{0:T(512)} %g1.1, bf16[9,16,21]{2,1,0:T(8,128)(2,1)} %bitcast.8, ...), custom_call_target="tpu_custom_call" | custom-call | flops 3000000000 | bytes 9000000 | tf_op jit(solution)/shard_map/pallas_call | solution.py:486
  34.7 1.8 %copy.15 = bf16[16,24,512]{2,1,0:T(8,128)(2,1)} copy(bf16[16,24,512]{2,1,0:T(8,128)(2,1)} %bitcast.5) | data formatting | bytes 786432

commit v2 on v1

--- a/solution.py
+++ b/solution.py
@@ -32,7 +32,7 @@
 bf16, f32 = jnp.bfloat16, jnp.float32
 MESH = pl.DeviceIdType.MESH
 
-HALF = IN_ROWS // 2
+EARLY = 12
 NEAR = [(0, -1), (0, 1), (0, -1), (0, 1)] + [(dy, dx) for dy in (-1, 1) for dx in (-1, 0, 1)]
 FROM_ROWS = {-1: 0, 1: IN_ROWS - EDGE_ROWS}
 TO_ROWS = {-1: EDGE_ROWS + IN_ROWS, 1: 0}
@@ -64,8 +64,8 @@
     x, foot, cke, cmat, coff, g1, nk, pol, mix, g2, emat, eoff, kmat,
     out,
     xe, footv, ckev, cmv, coffv, g1v, nkv, polv, mixv, g2v, ematv, eoffv, kmatv,
-    entv, tapv, polf, poltaps, lines, cmp, w, b, nv, lat, filt, gath, lhs, pres,
-    local_sem, near_send, near_recv, cap_send, cap_recv, hand_send, hand_recv,
+    entv, tapv, polf, poltaps, lines, cmp, w, b, nv, lat, filt, gath, lhs, pres, outv,
+    local_sem, near_send, near_recv, cap_send, cap_recv, hand_send, hand_recv, out_sem,
 ):
     la, lo = lax.axis_index("lat"), lax.axis_index("lon")
     north = la == 0
@@ -130,10 +130,10 @@
         dy, dx = NEAR[n]
         c0, cn = FROM_COLS[dx]
         if n < 2:
-            r0, rn = jnp.where(upper, 0, HALF), HALF
+            r0, rn = jnp.where(upper, 0, IN_ROWS - EARLY), EARLY
             to = r0 + EDGE_ROWS
         elif n < 4:
-            r0, rn = jnp.where(upper, HALF, 0), HALF
+            r0, rn = jnp.where(upper, EARLY, 0), IN_ROWS - EARLY
             to = r0 + EDGE_ROWS
         else:
             r0, rn, to = FROM_ROWS[dy], EDGE_ROWS, TO_ROWS[dy]
@@ -159,7 +159,7 @@
                             act(near(n))
 
     each_near(lambda c: c.start(), 1, 0, 10)
-    for n in (CM, COFF, G1, POL, G2, EOFF, MIX, EMAT, KMAT):
+    for n in (POL, CM, COFF, G1, G2, EOFF, MIX, EMAT, KMAT):
         local[n].start()
 
     @pl.when(north)
@@ -201,24 +201,30 @@
             [toeplitz(dense[k : k + 1], GROUP, 0, 2) for k in range(BASIS)], axis=0
         ).astype(bf16)
 
-    s = lax.broadcasted_iota(jnp.int32, (RLOC * LLOC, 128), 0)
-    lane = lax.broadcasted_iota(jnp.int32, (RLOC * LLOC, 128), 1)
-    spread = jnp.where(
-        ((lane & 31) < LLOC) & ((lane >> 5) * LLOC + (lane & 31) == s), 1.0, 0.0
-    ).astype(bf16)
-    for k in range(BASIS):
-        tapv[k] = jnp.dot(nkv[k], spread, preferred_element_type=f32)
-
-    @pl.loop(0, ROWS)
-    def _(i):
-        b[i] = jnp.concatenate(
-            [toeplitz(tapv[k, pl.ds(i, 1), :], COLS, 0, 1) for k in range(BASIS)], axis=0
+    def local_filters():
+        s = lax.broadcasted_iota(jnp.int32, (RLOC * LLOC, 128), 0)
+        lane = lax.broadcasted_iota(jnp.int32, (RLOC * LLOC, 128), 1)
+        spread = jnp.where(
+            ((lane & 31) < LLOC) & ((lane >> 5) * LLOC + (lane & 31) == s), 1.0, 0.0
         ).astype(bf16)
+        for k in range(BASIS):
+            tapv[k] = jnp.dot(nkv[k], spread, preferred_element_type=f32)
+
+        @pl.loop(0, ROWS)
+        def _(i):
+            b[i] = jnp.concatenate(
+                [toeplitz(tapv[k, pl.ds(i, 1), :], COLS, 0, 1) for k in range(BASIS)], axis=0
+            ).astype(bf16)
 
     local[CM].wait()
     for k in range(BASIS):
         cmp[k * 128 : k * 128 + VARS, :] = cmv[k * VARS : (k + 1) * VARS, :]
         cmp[k * 128 + VARS : (k + 1) * 128, :] = jnp.zeros((128 - VARS, FEAT), bf16)
+
+    @pl.when(jnp.logical_not(polar))
+    def _():
+        local[POL].wait()
+        local_filters()
 
     for n in (COFF, G1, OWN):
         local[n].wait()
@@ -293,11 +299,9 @@
         )
 
     def pass_on(ms):
-        @pl.when(polar)
-        def _():
-            for m in ms:
-                cap(m).wait_recv()
-                hand(m).start()
+        for m in ms:
+            cap(m).wait_recv()
+            hand(m).start()
 
     each_near(lambda c: c.wait_recv(), -1, 0, 2)
 
@@ -315,13 +319,6 @@
             cap(m).start()
         hand(0).start()
         each_near(lambda c: c.wait_recv(), -1, 2, 10)
-
-    order = sorted(range(1, chips), key=lambda m: (min(m, chips - m), m))
-    third = -(-len(order) // 3)
-
-    @pl.loop(0, 2)
-    def _(n):
-        coarsen(first + 4 + 7 * n, 7)
 
     span = nlon * SLOT
 
@@ -370,14 +367,17 @@
             )
             lhs[pl.ds(pl.multiple_of(2 * COLS * n, 2 * COLS), 2 * COLS), :] = both.astype(bf16)
 
-    pass_on(order[:third])
+    def coarsen_rest():
+        @pl.loop(0, 2)
+        def _(n):
+            coarsen(first + 4 + 7 * n, 7)
 
     def filters(i, extra):
         rhs = nv[pl.ds(i, 4)].reshape(4 * EXT_COLS, FEAT)
         got = jnp.dot(b[i], rhs, preferred_element_type=f32)
         return got if extra is None else got + extra
 
-    def filter_pair(i, extra):
+    def filter_pair(i, extra=None):
         one = filters(i, None if extra is None else pres[extra])
         two = filters(i + 1, None if extra is None else pres[extra + 1])
         for k in range(BASIS):
@@ -392,7 +392,7 @@
     gain_two = g2v
 
     def finish(i, rows):
-        at = pl.ds(pl.multiple_of(i * COLS, 4 * COLS), rows * COLS)
+        at = pl.ds(pl.multiple_of(i * COLS, 2 * COLS), rows * COLS)
         residual = lat[pl.ds(i + 1, rows), 3 : 3 + COLS, :].reshape(rows * COLS, FEAT)
         middle = residual + jnp.dot(filt[at, :], mixv[...], preferred_element_type=f32)
         middle = middle.astype(bf16).astype(f32)
@@ -400,47 +400,80 @@
         hidden = jnp.dot(normed, ematv[...], preferred_element_type=f32)
         hidden = gelu(hidden + expand_offset[...].reshape(1, HIDDEN)).astype(bf16)
         encoded = middle + jnp.dot(hidden, kmatv[...], preferred_element_type=f32)
-        out[at, :] = encoded.astype(bf16)
-
-    big, small = jnp.where(upper, 4, 0), jnp.where(upper, 0, ROWS - 4)
-
-    @pl.loop(0, (ROWS - 4) // 2)
-    def _(n):
-        filter_pair(big + 2 * n, None)
-
-    pass_on(order[third : 2 * third])
-    for n in (G2, EOFF, MIX, EMAT, KMAT):
-        local[n].wait()
-    finish(big, ROWS - 4)
-    pass_on(order[2 * third :])
-
-    pres[...] = jnp.zeros(pres.shape, f32)
+        outv[at, :] = encoded.astype(bf16)
+
+    def store(part, i, rows):
+        at = pl.ds(pl.multiple_of(i * COLS, 2 * COLS), rows * COLS)
+        return pltpu.make_async_copy(outv.at[at], out.at[at], out_sem.at[part])
+
+    @pl.when(jnp.logical_not(polar))
+    def _():
+        coarsen_rest()
+
+        @pl.loop(0, ROWS // 2)
+        def _(n):
+            filter_pair(2 * n)
+
+        for n in (G2, EOFF, MIX, EMAT, KMAT):
+            local[n].wait()
+        finish(0, ROWS)
+        copy = store(0, 0, ROWS)
+        copy.start()
+        copy.wait()
 
     @pl.when(polar)
     def _():
+        big, small = jnp.where(north, 4, 0), jnp.where(north, 0, ROWS - 4)
+        near_by = sorted({1, chips - 1, chips // 2} - {0})
+        rest = [m for m in range(1, chips) if m not in near_by]
+        some = len(rest) // 2
+        local_filters()
+        coarsen_rest()
+        @pl.loop(0, (ROWS - 4) // 2)
+        def _(n):
+            filter_pair(big + 2 * n)
+
+        pass_on(near_by)
+        pass_on(rest)
+        for n in (G2, EOFF, MIX, EMAT, KMAT):
+            local[n].wait()
+        finish(big, 12)
+        store(0, big, 6).start()
+        store(1, big + 6, 6).start()
         for m in range(chips):
             hand(m, False).wait_recv()
+        got = jnp.dot(lhs[...], gath[...].reshape(span, FEAT), preferred_element_type=f32)
         lead = jnp.where(north, 0, 1)
-        got = jnp.dot(lhs[...], gath[...].reshape(span, FEAT), preferred_element_type=f32)
+        pres[jnp.where(north, 3, 0)] = jnp.zeros((BASIS * COLS, FEAT), f32)
         for t in range(CAP):
             pres[t + lead] = got[t * BASIS * COLS : (t + 1) * BASIS * COLS]
-
-    filter_pair(small, 0)
-    filter_pair(small + 2, 2)
-    finish(small, 4)
-
-    each_near(lambda c: c.wait_send(), 1, 0, 10)
-
-    @pl.when(polar)
-    def _():
+        filter_pair(small, 0)
+        filter_pair(small + 2, 2)
+        finish(small, 4)
+        store(2, small, 4).start()
         for m in range(1, chips):
             cap(m).wait_send()
         for m in range(chips):
             hand(m).wait_send()
-
-    @pl.when(jnp.logical_not(polar))
-    def _():
-        local[POL].wait()
+        store(0, big, 6).wait()
+        store(1, big + 6, 6).wait()
+        store(2, small, 4).wait()
+
+    each_near(lambda c: c.wait_send(), 1, 0, 10)
+
+
+def copy_kernel(source, out, sem):
+    rows = source.shape[0] // 4
+    parts = [
+        pltpu.make_async_copy(
+            source.at[pl.ds(n * rows, rows)], out.at[pl.ds(n * rows, rows)], sem.at[n]
+        )
+        for n in range(4)
+    ]
+    for part in parts:
+        part.start()
+    for part in parts:
+        part.wait()
 
 
 def body(x, foot, cke, cmat, coff, g1, nk, pol, mix, g2, emat, eoff, kmat):
@@ -475,6 +508,7 @@
         vmem((nlon, SLOT, FEAT), bf16),
         vmem(((CAP * BASIS + 1) * COLS, span), bf16),
         vmem((4, BASIS * COLS, FEAT), f32),
+        vmem((ROWS * COLS, FEAT), bf16),
         pltpu.SemaphoreType.DMA((13,)),
         pltpu.SemaphoreType.DMA((10,)),
         pltpu.SemaphoreType.DMA((10,)),
@@ -482,12 +516,13 @@
         pltpu.SemaphoreType.DMA((nlon // 2 - 1,)),
         pltpu.SemaphoreType.DMA((nlon // 2,)),
         pltpu.SemaphoreType.DMA((nlon // 2,)),
+        pltpu.SemaphoreType.DMA((3,)),
     ]
     encoded = pl.pallas_call(
         functools.partial(kernel, nlat, nlon),
         out_shape=jax.ShapeDtypeStruct((ROWS * COLS, FEAT), bf16),
         in_specs=[pl.BlockSpec(memory_space=pl.ANY)] * 13,
-        out_specs=pl.BlockSpec(memory_space=pltpu.VMEM),
+        out_specs=pl.BlockSpec(memory_space=pl.ANY),
         scratch_shapes=scratch,
         compiler_params=pltpu.CompilerParams(
             collective_id=0, has_side_effects=True, vmem_limit_bytes=56 << 20

time: 36.8 us -> 32 us (0.87)
  Pallas kernels: 34.7 us -> 29.7 us
    pallas_call x1, Pallas kernels: 34.7 us -> 29.7 us  [body(): pl.pallas_call(functools.partial(kernel, nlat, nlon), out_shape=jax.Shape...]
where the time goes in v2:
time: 32 us; the launch traced here: 31.5 us
  Pallas kernels  29.7 us (93%)
  local copies, waits for them, and re-layouts  1.77 us (6%)
    pallas_call x1, Pallas kernels, body(): pl.pallas_call(functools.partial(kernel, nlat, nlon), out_shape=jax.Shape...  29.7 us
    unnamed x1, local copies, waits for them, and re-layouts  1.77 us

profile of v2, /device:TPU:1, one launch (start us, length us, event | category | flops | bytes accessed | tf_op | source)
XLA Modules:
  0.0 31.5 jit_solution(16337912272914497575)
XLA Ops:
  0.0 29.7 %shard_map.127 = bf16[384,512]{1,0:T(8,128)(2,1)} custom-call(bf16[32,48,72]{2,1,0:T(8,128)(2,1)} %x.1, s32[32,128]{1,0:T(8,128)} %bitcast.9, bf16[9,32,128]{2,1,0:T(8,128)(2,1)} %bitcast.7, bf16[648,512]{1,0:T(8,128)(2,1)} %cmat.1, f32[512]{0:T(512)} %coff.1, f32[512]{0:T(512)} %g1.1, bf16[9,16,21]{2,1,0:T(8,128)(2,1)} %bitcast.8, ...), custom_call_target="tpu_custom_call" | custom-call | flops 3000000000 | bytes 9000000 | tf_op jit(solution)/shard_map/pallas_call | solution.py:521
  29.7 1.8 %copy.15 = bf16[16,24,512]{2,1,0:T(8,128)(2,1)} copy(bf16[16,24,512]{2,1,0:T(8,128)(2,1)} %bitcast.5) | data formatting | bytes 786432

commit v3 on v2

--- a/solution.py
+++ b/solution.py
@@ -28,6 +28,10 @@
 EXT_ROWS = ROWS + 2
 EXT_COLS = 32
 SLOT = 4 * COLS
+INNER = 20
+FRONT = 4 * INNER
+QUAD = 4 * COLS
+PAD_ROWS = 224
 EPS = 1e-05
 bf16, f32 = jnp.bfloat16, jnp.float32
 MESH = pl.DeviceIdType.MESH
@@ -64,8 +68,8 @@
     x, foot, cke, cmat, coff, g1, nk, pol, mix, g2, emat, eoff, kmat,
     out,
     xe, footv, ckev, cmv, coffv, g1v, nkv, polv, mixv, g2v, ematv, eoffv, kmatv,
-    entv, tapv, polf, poltaps, lines, cmp, w, b, nv, lat, filt, gath, lhs, pres, outv,
-    local_sem, near_send, near_recv, cap_send, cap_recv, hand_send, hand_recv, out_sem,
+    entv, tapv, polf, sort, taps, cmp, w, b, nv, lat, filt, gath, lhs, pres,
+    local_sem, near_send, near_recv, cap_send, cap_recv, hand_send, hand_recv,
 ):
     la, lo = lax.axis_index("lat"), lax.axis_index("lon")
     north = la == 0
@@ -118,7 +122,7 @@
     ]
     FOOT, CKE, NK, OWN, CM, COFF, G1, POL, G2, EOFF, MIX, EMAT, KMAT = range(13)
     local = [pltpu.make_async_copy(s, d, local_sem.at[n]) for n, (s, d) in enumerate(pairs)]
-    for n in (FOOT, CKE, NK, OWN):
+    for n in (FOOT, CKE, OWN, CM, COFF, G1, NK, POL):
         local[n].start()
 
     pl.semaphore_wait(
@@ -159,7 +163,7 @@
                             act(near(n))
 
     each_near(lambda c: c.start(), 1, 0, 10)
-    for n in (POL, CM, COFF, G1, G2, EOFF, MIX, EMAT, KMAT):
+    for n in (G2, EOFF, MIX, EMAT, KMAT):
         local[n].start()
 
     @pl.when(north)
@@ -188,8 +192,10 @@
     cycle = lax.broadcasted_iota(jnp.int32, (CELLS, total), 1)
     place = lax.broadcasted_iota(jnp.int32, (CELLS, 256), 1).astype(f32)
 
-    @pl.loop(0, EXT_ROWS)
-    def _(i):
+    first = jnp.where(upper, 1, ROWS - 3)
+
+    def banded(n):
+        i = lax.rem(first + n, EXT_ROWS)
         cells = footv[...]
         lanes = (cells + (WINDOW - LWIN) * ((cells * 205) >> 11) + 6).astype(f32)
         column = jnp.sum(
@@ -200,6 +206,8 @@
         w[i] = jnp.concatenate(
             [toeplitz(dense[k : k + 1], GROUP, 0, 2) for k in range(BASIS)], axis=0
         ).astype(bf16)
+
+    pl.loop(0, 4)(banded)
 
     def local_filters():
         s = lax.broadcasted_iota(jnp.int32, (RLOC * LLOC, 128), 0)
@@ -221,23 +229,22 @@
         cmp[k * 128 : k * 128 + VARS, :] = cmv[k * VARS : (k + 1) * VARS, :]
         cmp[k * 128 + VARS : (k + 1) * 128, :] = jnp.zeros((128 - VARS, FEAT), bf16)
 
-    @pl.when(jnp.logical_not(polar))
-    def _():
-        local[POL].wait()
-        local_filters()
-
-    for n in (COFF, G1, OWN):
+    for n in (COFF, G1, OWN, POL):
         local[n].wait()
 
-    first = jnp.where(upper, 1, ROWS - 3)
     offset = coffv[...].reshape(1, FEAT)
     gain = g1v[...].reshape(1, FEAT)
 
-    def coarsen(begin, count):
+    def coarsen(begin, count, sides=True):
         parts = []
         for m in range(count):
             i = lax.rem(begin + m, EXT_ROWS)
-            rows = xe[pl.ds(2 * i, RIN)]
+            if sides:
+                rows = xe[pl.ds(2 * i, RIN)]
+            else:
+                none = jnp.zeros((RIN, EDGE_COLS, VARS), bf16)
+                own = xe[pl.ds(2 * i, RIN), EDGE_COLS : EDGE_COLS + IN_COLS]
+                rows = jnp.concatenate([none, own, none], axis=1)
             windows = [
                 jnp.concatenate(
                     [
@@ -268,6 +275,8 @@
         )
         latent = (latent + offset).astype(bf16).astype(f32)
         normed = norm(latent, gain)
+        if not sides:
+            return normed
         for m in range(count):
             i = lax.rem(begin + m, EXT_ROWS)
             g = la * ROWS + i - 1
@@ -276,12 +285,13 @@
             nv[i] = jnp.where((g >= 0) & (g < total), row, 0.0).astype(bf16)
         return normed
 
-    def cap(m):
+    def cap(m, late):
+        at = pl.ds(FRONT, SLOT - FRONT) if late else pl.ds(0, FRONT)
         return pltpu.make_async_remote_copy(
-            src_ref=gath.at[0],
-            dst_ref=gath.at[nlon - 2 * m],
-            send_sem=cap_send.at[m - 1],
-            recv_sem=cap_recv.at[m - 1],
+            src_ref=gath.at[0, at],
+            dst_ref=gath.at[nlon - 2 * m, at],
+            send_sem=cap_send.at[late, m - 1],
+            recv_sem=cap_recv.at[late, m - 1],
             device_id=(la, lax.rem(lo + 2 * m, nlon)),
             device_id_type=MESH,
         )
@@ -300,41 +310,43 @@
 
     def pass_on(ms):
         for m in ms:
-            cap(m).wait_recv()
+            cap(m, 0).wait_recv()
+            cap(m, 1).wait_recv()
             hand(m).start()
 
-    each_near(lambda c: c.wait_recv(), -1, 0, 2)
-
-    @pl.when(jnp.logical_not(polar))
-    def _():
-        each_near(lambda c: c.wait_recv(), -1, 2, 10)
-
-    normed = coarsen(first, 4)
-
     @pl.when(polar)
     def _():
-        rows = [normed[m * EXT_COLS + 3 : m * EXT_COLS + 3 + COLS] for m in range(4)]
-        gath[0] = jnp.concatenate(rows, axis=0).astype(bf16)
-        for m in range(1, chips):
-            cap(m).start()
-        hand(0).start()
-        each_near(lambda c: c.wait_recv(), -1, 2, 10)
-
+        normed = coarsen(first, 4, False)
+        rows = [normed[m * EXT_COLS + 5 : m * EXT_COLS + 5 + INNER] for m in range(4)]
+        gath[0, 0:FRONT] = jnp.concatenate(rows, axis=0).astype(bf16)
+        for m in (2, 6, 3, 5, 1, 7, 4):
+            cap(m, 0).start()
+
+    pl.loop(4, EXT_ROWS)(banded)
+
+    quads = nlon // 4
     span = nlon * SLOT
 
-    @pl.when(polar)
-    def _():
-        local[POL].wait()
-        lane = lax.broadcasted_iota(jnp.int32, (1, span), 1)
+    def polar_taps():
+        lane = lax.broadcasted_iota(jnp.int32, (1, 4 * SLOT), 1)
         dev = lane // SLOT
-        inner = lane - dev * SLOT
-        cycle = inner // COLS
-        inner = inner - cycle * COLS
-        source = jnp.where(cycle == 0, dev * COLS + inner, -1)
-        pick = jnp.where(
-            lax.broadcasted_iota(jnp.int32, (nlon * COLS, span), 0) == source, 1.0, 0.0
-        ).astype(bf16)
+        place = lane - dev * SLOT
+        front = place < FRONT
+        side = place - FRONT
+        cycle = jnp.where(front, place // INNER, side // 4)
+        end = side - 4 * (side // 4)
+        inner = jnp.where(
+            front, place - cycle * INNER + 2, jnp.where(end < 2, end, end + INNER)
+        )
         lead = jnp.where(north, 1, 0)
+        for t in range(CAP):
+            r = cycle - t + lead
+            source = jnp.where(
+                (r >= 0) & (r < RLOC), r * 128 + dev * COLS + inner, -1
+            )
+            sort[t] = jnp.where(
+                lax.broadcasted_iota(jnp.int32, (RLOC * 128, 4 * SLOT), 0) == source, 1.0, 0.0
+            ).astype(bf16)
         polf[...] = jnp.zeros(polf.shape, f32)
         for t in range(CAP):
             for r in range(RLOC):
@@ -342,35 +354,63 @@
                     both = polv[t, k, r].astype(f32)
                     n = (t * RLOC + r) * 16 + k
                     polf[n : n + 1, :] = jnp.where(north, both[0:1], both[1:2])
-        poltaps[...] = jnp.dot(polf[...].astype(bf16), pick, preferred_element_type=f32)
-        for t in range(CAP):
-            line = jnp.zeros((16, span), f32)
-            for r in range(RLOC):
-                n = (t * RLOC + r) * 16
-                to = t + r - lead
-                moved = pltpu.roll(poltaps[n : n + 16, :], lax.rem(COLS * to + span, span), 1)
-                line = line + jnp.where(cycle == to, moved, 0.0)
-            lines[t * 16 : (t + 1) * 16, :] = line
-        inside = inner >= lax.broadcasted_iota(jnp.int32, (COLS, span), 0)
-
-        def circulant(n):
-            t = n // BASIS
-            line = lines[pl.ds(t * 16 + n - t * BASIS, 1), :]
-            return jnp.where(
-                inside, toeplitz(line, COLS, 0, 1), toeplitz(line, COLS, SLOT - COLS, 1)
-            )
-
-        @pl.loop(0, (CAP * BASIS + 1) // 2)
-        def _(n):
-            both = jnp.concatenate(
-                [circulant(2 * n), circulant(jnp.minimum(2 * n + 1, CAP * BASIS - 1))], axis=0
-            )
-            lhs[pl.ds(pl.multiple_of(2 * COLS * n, 2 * COLS), 2 * COLS), :] = both.astype(bf16)
-
-    def coarsen_rest():
-        @pl.loop(0, 2)
-        def _(n):
-            coarsen(first + 4 + 7 * n, 7)
+        at = lax.broadcasted_iota(jnp.int32, (16, 128), 1)
+        length = nlon * COLS
+        for n in range(CAP * RLOC):
+            line = polf[n * 16 : (n + 1) * 16, :]
+            for q in range(quads):
+                ahead = pltpu.roll(line, (length - QUAD * q) % length, 1)[:, :128]
+                before = pltpu.roll(line, (length + 128 - QUAD * q) % length, 1)[:, :128]
+                taps[n, q] = jnp.where(
+                    at < QUAD, ahead, jnp.where(at >= 128 - COLS, before, 0.0)
+                )
+
+    def circulants():
+        @pl.loop(0, quads)
+        def _(q):
+            for t in range(CAP):
+                rows = []
+                for k in range(BASIS):
+                    rows.append(
+                        jnp.concatenate(
+                            [
+                                toeplitz(taps[t * RLOC + r, q, k : k + 1, :], COLS, 0, 1)
+                                for r in range(RLOC)
+                            ],
+                            axis=1,
+                        )
+                    )
+                block = jnp.dot(
+                    jnp.concatenate(rows, axis=0).astype(bf16),
+                    sort[t],
+                    preferred_element_type=f32,
+                )
+                lhs[
+                    t * PAD_ROWS : t * PAD_ROWS + BASIS * COLS,
+                    pl.ds(pl.multiple_of(4 * SLOT * q, 128), 4 * SLOT),
+                ] = block.astype(bf16)
+
+    @pl.when(jnp.logical_not(polar))
+    def _():
+        local_filters()
+
+    @pl.when(polar)
+    def _():
+        polar_taps()
+
+    each_near(lambda c: c.wait_recv(), -1, 0, 2)
+
+    @pl.when(polar)
+    def _():
+        normed = coarsen(first, 4)
+        rows = []
+        for m in range(4):
+            rows.append(normed[m * EXT_COLS + 3 : m * EXT_COLS + 5])
+            rows.append(normed[m * EXT_COLS + 5 + INNER : m * EXT_COLS + 7 + INNER])
+        gath[0, FRONT:SLOT] = jnp.concatenate(rows, axis=0).astype(bf16)
+        for m in (2, 6, 3, 5, 1, 7, 4):
+            cap(m, 1).start()
+        hand(0).start()
 
     def filters(i, extra):
         rhs = nv[pl.ds(i, 4)].reshape(4 * EXT_COLS, FEAT)
@@ -400,15 +440,18 @@
         hidden = jnp.dot(normed, ematv[...], preferred_element_type=f32)
         hidden = gelu(hidden + expand_offset[...].reshape(1, HIDDEN)).astype(bf16)
         encoded = middle + jnp.dot(hidden, kmatv[...], preferred_element_type=f32)
-        outv[at, :] = encoded.astype(bf16)
-
-    def store(part, i, rows):
-        at = pl.ds(pl.multiple_of(i * COLS, 2 * COLS), rows * COLS)
-        return pltpu.make_async_copy(outv.at[at], out.at[at], out_sem.at[part])
+        out[at, :] = encoded.astype(bf16)
 
     @pl.when(jnp.logical_not(polar))
     def _():
-        coarsen_rest()
+        each_near(lambda c: c.wait_recv(), -1, 2, 4)
+
+        @pl.loop(0, 2)
+        def _(n):
+            coarsen(2 + 7 * n, 7)
+
+        each_near(lambda c: c.wait_recv(), -1, 4, 10)
+        coarsen(ROWS, 4)
 
         @pl.loop(0, ROWS // 2)
         def _(n):
@@ -417,63 +460,44 @@
         for n in (G2, EOFF, MIX, EMAT, KMAT):
             local[n].wait()
         finish(0, ROWS)
-        copy = store(0, 0, ROWS)
-        copy.start()
-        copy.wait()
 
     @pl.when(polar)
     def _():
         big, small = jnp.where(north, 4, 0), jnp.where(north, 0, ROWS - 4)
-        near_by = sorted({1, chips - 1, chips // 2} - {0})
-        rest = [m for m in range(1, chips) if m not in near_by]
-        some = len(rest) // 2
+        circulants()
         local_filters()
-        coarsen_rest()
+        each_near(lambda c: c.wait_recv(), -1, 2, 10)
+
+        @pl.loop(0, 2)
+        def _(n):
+            coarsen(first + 4 + 7 * n, 7)
+
         @pl.loop(0, (ROWS - 4) // 2)
         def _(n):
             filter_pair(big + 2 * n)
 
-        pass_on(near_by)
-        pass_on(rest)
+        pass_on(range(1, chips))
         for n in (G2, EOFF, MIX, EMAT, KMAT):
             local[n].wait()
-        finish(big, 12)
-        store(0, big, 6).start()
-        store(1, big + 6, 6).start()
+        finish(big, ROWS - 4)
+
         for m in range(chips):
             hand(m, False).wait_recv()
         got = jnp.dot(lhs[...], gath[...].reshape(span, FEAT), preferred_element_type=f32)
         lead = jnp.where(north, 0, 1)
         pres[jnp.where(north, 3, 0)] = jnp.zeros((BASIS * COLS, FEAT), f32)
         for t in range(CAP):
-            pres[t + lead] = got[t * BASIS * COLS : (t + 1) * BASIS * COLS]
+            pres[t + lead] = got[t * PAD_ROWS : t * PAD_ROWS + BASIS * COLS]
         filter_pair(small, 0)
         filter_pair(small + 2, 2)
         finish(small, 4)
-        store(2, small, 4).start()
         for m in range(1, chips):
-            cap(m).wait_send()
+            cap(m, 0).wait_send()
+            cap(m, 1).wait_send()
         for m in range(chips):
             hand(m).wait_send()
-        store(0, big, 6).wait()
-        store(1, big + 6, 6).wait()
-        store(2, small, 4).wait()
 
     each_near(lambda c: c.wait_send(), 1, 0, 10)
-
-
-def copy_kernel(source, out, sem):
-    rows = source.shape[0] // 4
-    parts = [
-        pltpu.make_async_copy(
-            source.at[pl.ds(n * rows, rows)], out.at[pl.ds(n * rows, rows)], sem.at[n]
-        )
-        for n in range(4)
-    ]
-    for part in parts:
-        part.start()
-    for part in parts:
-        part.wait()
 
 
 def body(x, foot, cke, cmat, coff, g1, nk, pol, mix, g2, emat, eoff, kmat):
@@ -497,8 +521,8 @@
         vmem((EXT_ROWS, BASIS, CELLS), f32),
         vmem((BASIS, ROWS, 128), f32),
         vmem((CAP * RLOC * 16, nlon * COLS), f32),
-        vmem((CAP * RLOC * 16, span), f32),
-        vmem((CAP * 16, span), f32),
+        vmem((CAP, RLOC * 128, 4 * SLOT), bf16),
+        vmem((CAP * RLOC, nlon // 4, 16, 128), f32),
         vmem((BASIS * 128, FEAT), bf16),
         vmem((EXT_ROWS, BASIS * GROUP, 256), bf16),
         vmem((ROWS, BASIS * COLS, 128), bf16),
@@ -506,23 +530,21 @@
         vmem((EXT_ROWS, EXT_COLS, FEAT), f32),
         vmem((ROWS * COLS, BASIS * FEAT), bf16),
         vmem((nlon, SLOT, FEAT), bf16),
-        vmem(((CAP * BASIS + 1) * COLS, span), bf16),
+        vmem((CAP * PAD_ROWS, span), bf16),
         vmem((4, BASIS * COLS, FEAT), f32),
-        vmem((ROWS * COLS, FEAT), bf16),
         pltpu.SemaphoreType.DMA((13,)),
         pltpu.SemaphoreType.DMA((10,)),
         pltpu.SemaphoreType.DMA((10,)),
-        pltpu.SemaphoreType.DMA((nlon // 2 - 1,)),
-        pltpu.SemaphoreType.DMA((nlon // 2 - 1,)),
+        pltpu.SemaphoreType.DMA((2, nlon // 2 - 1)),
+        pltpu.SemaphoreType.DMA((2, nlon // 2 - 1)),
         pltpu.SemaphoreType.DMA((nlon // 2,)),
         pltpu.SemaphoreType.DMA((nlon // 2,)),
-        pltpu.SemaphoreType.DMA((3,)),
     ]
     encoded = pl.pallas_call(
         functools.partial(kernel, nlat, nlon),
-        out_shape=jax.ShapeDtypeStruct((ROWS * COLS, FEAT), bf16),
+        out_shape=pltpu.VMEM((ROWS * COLS, FEAT), bf16),
         in_specs=[pl.BlockSpec(memory_space=pl.ANY)] * 13,
-        out_specs=pl.BlockSpec(memory_space=pl.ANY),
+        out_specs=pl.BlockSpec(memory_space=pltpu.VMEM),
         scratch_shapes=scratch,
         compiler_params=pltpu.CompilerParams(
             collective_id=0, has_side_effects=True, vmem_limit_bytes=56 << 20

time: 32 us -> 28.9 us (0.903); the launches traced: 31.5 us -> 28.8 us
  Pallas kernels: 29.7 us -> 28.1 us
  local copies, waits for them, and re-layouts: 1.77 us -> 0.75 us
    pallas_call x1, Pallas kernels: 29.7 us -> 28.1 us  [body(): pl.pallas_call(functools.partial(kernel, nlat, nlon), out_shape=pltpu.VME...]
    unnamed x1, local copies, waits for them, and re-layouts: 1.77 us -> 0.75 us
where the time goes in v3:
time: 28.9 us; the launch traced here: 28.8 us
  Pallas kernels  28.1 us (97%)
  local copies, waits for them, and re-layouts  0.75 us (3%)
    pallas_call x1, Pallas kernels, body(): pl.pallas_call(functools.partial(kernel, nlat, nlon), out_shape=pltpu.VME...  28.1 us
    unnamed x1, local copies, waits for them, and re-layouts  0.75 us

profile of v3, /device:TPU:1, one launch (start us, length us, event | category | flops | bytes accessed | tf_op | source)
XLA Modules:
  0.0 28.8 jit_solution(18115442961109842419)
XLA Ops:
  0.0 28.1 %shard_map.127 = bf16[384,512]{1,0:T(8,128)(2,1)S(1)} custom-call(bf16[32,48,72]{2,1,0:T(8,128)(2,1)} %x.1, s32[32,128]{1,0:T(8,128)} %bitcast.9, bf16[9,32,128]{2,1,0:T(8,128)(2,1)} %bitcast.7, bf16[648,512]{1,0:T(8,128)(2,1)} %cmat.1, f32[512]{0:T(512)} %coff.1, f32[512]{0:T(512)} %g1.1, bf16[9,16,21]{2,1,0:T(8,128)(2,1)} %bitcast.8, ...), custom_call_target="tpu_custom_call" | custom-call | flops 3000000000 | bytes 9000000 | tf_op jit(solution)/shard_map/pallas_call | solution.py:543
  28.1 0.7 %copy.15 = bf16[16,24,512]{2,1,0:T(8,128)(2,1)} copy(bf16[16,24,512]{2,1,0:T(8,128)(2,1)S(1)} %bitcast.5) | data formatting | bytes 786432

commit v4 on v3

--- a/solution.py
+++ b/solution.py
@@ -125,11 +125,6 @@
     for n in (FOOT, CKE, OWN, CM, COFF, G1, NK, POL):
         local[n].start()
 
-    pl.semaphore_wait(
-        barrier,
-        2 + jnp.where(polar, chips - 1, 0) + jnp.where(north, 0, 3) + jnp.where(south, 0, 3),
-    )
-
     def near(n):
         dy, dx = NEAR[n]
         c0, cn = FROM_COLS[dx]
@@ -162,10 +157,6 @@
                         if NEAR[n][0] == dy:
                             act(near(n))
 
-    each_near(lambda c: c.start(), 1, 0, 10)
-    for n in (G2, EOFF, MIX, EMAT, KMAT):
-        local[n].start()
-
     @pl.when(north)
     def _():
         xe[0:EDGE_ROWS] = jnp.zeros((EDGE_ROWS, WIDE, VARS), bf16)
@@ -207,7 +198,7 @@
             [toeplitz(dense[k : k + 1], GROUP, 0, 2) for k in range(BASIS)], axis=0
         ).astype(bf16)
 
-    pl.loop(0, 4)(banded)
+    pl.loop(0, 4, unroll=4)(banded)
 
     def local_filters():
         s = lax.broadcasted_iota(jnp.int32, (RLOC * LLOC, 128), 0)
@@ -218,7 +209,7 @@
         for k in range(BASIS):
             tapv[k] = jnp.dot(nkv[k], spread, preferred_element_type=f32)
 
-        @pl.loop(0, ROWS)
+        @pl.loop(0, ROWS, unroll=4)
         def _(i):
             b[i] = jnp.concatenate(
                 [toeplitz(tapv[k, pl.ds(i, 1), :], COLS, 0, 1) for k in range(BASIS)], axis=0
@@ -285,8 +276,13 @@
             nv[i] = jnp.where((g >= 0) & (g < total), row, 0.0).astype(bf16)
         return normed
 
+    sending = sorted(range(1, chips), key=lambda m: (abs(abs(2 * m - chips) - chips // 2), m))
+
+    def part(late):
+        return pl.ds(FRONT, SLOT - FRONT) if late else pl.ds(0, FRONT)
+
     def cap(m, late):
-        at = pl.ds(FRONT, SLOT - FRONT) if late else pl.ds(0, FRONT)
+        at = part(late)
         return pltpu.make_async_remote_copy(
             src_ref=gath.at[0, at],
             dst_ref=gath.at[nlon - 2 * m, at],
@@ -296,33 +292,44 @@
             device_id_type=MESH,
         )
 
-    def hand(m, out=True):
+    def hand(m, late, out=True):
         slot = (nlon - 2 * m) % nlon
         west = jnp.where(core == 0, nlon - 1, 1) if out else jnp.where(core == 0, 1, nlon - 1)
         return pltpu.make_async_remote_copy(
-            src_ref=gath.at[slot],
-            dst_ref=gath.at[lax.rem(slot + west, nlon)],
-            send_sem=hand_send.at[m],
-            recv_sem=hand_recv.at[m],
+            src_ref=gath.at[slot, part(late)],
+            dst_ref=gath.at[lax.rem(slot + west, nlon), part(late)],
+            send_sem=hand_send.at[late, m],
+            recv_sem=hand_recv.at[late, m],
             device_id=(la, sibling),
             device_id_type=MESH,
         )
 
-    def pass_on(ms):
-        for m in ms:
-            cap(m, 0).wait_recv()
-            cap(m, 1).wait_recv()
-            hand(m).start()
+    def pass_on(late):
+        for m in sending:
+            cap(m, late).wait_recv()
+            hand(m, late).start()
 
     @pl.when(polar)
     def _():
         normed = coarsen(first, 4, False)
         rows = [normed[m * EXT_COLS + 5 : m * EXT_COLS + 5 + INNER] for m in range(4)]
         gath[0, 0:FRONT] = jnp.concatenate(rows, axis=0).astype(bf16)
-        for m in (2, 6, 3, 5, 1, 7, 4):
+
+    pl.semaphore_wait(
+        barrier,
+        2 + jnp.where(polar, chips - 1, 0) + jnp.where(north, 0, 3) + jnp.where(south, 0, 3),
+    )
+
+    each_near(lambda c: c.start(), 1, 0, 10)
+    @pl.when(polar)
+    def _():
+        for m in sending:
             cap(m, 0).start()
 
-    pl.loop(4, EXT_ROWS)(banded)
+    for n in (G2, EOFF, MIX, EMAT, KMAT):
+        local[n].start()
+
+    pl.loop(4, EXT_ROWS, unroll=7)(banded)
 
     quads = nlon // 4
     span = nlon * SLOT
@@ -366,7 +373,7 @@
                 )
 
     def circulants():
-        @pl.loop(0, quads)
+        @pl.loop(0, quads, unroll=4)
         def _(q):
             for t in range(CAP):
                 rows = []
@@ -408,9 +415,10 @@
             rows.append(normed[m * EXT_COLS + 3 : m * EXT_COLS + 5])
             rows.append(normed[m * EXT_COLS + 5 + INNER : m * EXT_COLS + 7 + INNER])
         gath[0, FRONT:SLOT] = jnp.concatenate(rows, axis=0).astype(bf16)
-        for m in (2, 6, 3, 5, 1, 7, 4):
+        for m in sending:
             cap(m, 1).start()
-        hand(0).start()
+        hand(0, 0).start()
+        hand(0, 1).start()
 
     def filters(i, extra):
         rhs = nv[pl.ds(i, 4)].reshape(4 * EXT_COLS, FEAT)
@@ -453,7 +461,7 @@
         each_near(lambda c: c.wait_recv(), -1, 4, 10)
         coarsen(ROWS, 4)
 
-        @pl.loop(0, ROWS // 2)
+        @pl.loop(0, ROWS // 2, unroll=2)
         def _(n):
             filter_pair(2 * n)
 
@@ -472,17 +480,20 @@
         def _(n):
             coarsen(first + 4 + 7 * n, 7)
 
-        @pl.loop(0, (ROWS - 4) // 2)
+        @pl.loop(0, (ROWS - 4) // 2, unroll=2)
         def _(n):
             filter_pair(big + 2 * n)
 
-        pass_on(range(1, chips))
         for n in (G2, EOFF, MIX, EMAT, KMAT):
             local[n].wait()
-        finish(big, ROWS - 4)
+        finish(big, 6)
+        pass_on(0)
+        pass_on(1)
+        finish(big + 6, 6)
 
         for m in range(chips):
-            hand(m, False).wait_recv()
+            hand(m, 0, False).wait_recv()
+            hand(m, 1, False).wait_recv()
         got = jnp.dot(lhs[...], gath[...].reshape(span, FEAT), preferred_element_type=f32)
         lead = jnp.where(north, 0, 1)
         pres[jnp.where(north, 3, 0)] = jnp.zeros((BASIS * COLS, FEAT), f32)
@@ -495,7 +506,8 @@
             cap(m, 0).wait_send()
             cap(m, 1).wait_send()
         for m in range(chips):
-            hand(m).wait_send()
+            hand(m, 0).wait_send()
+            hand(m, 1).wait_send()
 
     each_near(lambda c: c.wait_send(), 1, 0, 10)
 
@@ -537,8 +549,8 @@
         pltpu.SemaphoreType.DMA((10,)),
         pltpu.SemaphoreType.DMA((2, nlon // 2 - 1)),
         pltpu.SemaphoreType.DMA((2, nlon // 2 - 1)),
-        pltpu.SemaphoreType.DMA((nlon // 2,)),
-        pltpu.SemaphoreType.DMA((nlon // 2,)),
+        pltpu.SemaphoreType.DMA((2, nlon // 2)),
+        pltpu.SemaphoreType.DMA((2, nlon // 2)),
     ]
     encoded = pl.pallas_call(
         functools.partial(kernel, nlat, nlon),

time: 28.9 us -> 27.9 us (0.965)
  Pallas kernels: 28.1 us -> 27 us
    pallas_call x1, Pallas kernels: 28.1 us -> 27 us  [body(): pl.pallas_call(functools.partial(kernel, nlat, nlon), out_shape=pltpu.VME...]
where the time goes in v4:
time: 27.9 us; the launch traced here: 27.8 us
  Pallas kernels  27 us (97%)
  local copies, waits for them, and re-layouts  0.75 us (3%)
    pallas_call x1, Pallas kernels, body(): pl.pallas_call(functools.partial(kernel, nlat, nlon), out_shape=pltpu.VME...  27 us
    unnamed x1, local copies, waits for them, and re-layouts  0.75 us

profile of v4, /device:TPU:1, one launch (start us, length us, event | category | flops | bytes accessed | tf_op | source)
XLA Modules:
  0.0 27.8 jit_solution(9253629356398686342)
XLA Ops:
  0.0 27.0 %shard_map.127 = bf16[384,512]{1,0:T(8,128)(2,1)S(1)} custom-call(bf16[32,48,72]{2,1,0:T(8,128)(2,1)} %x.1, s32[32,128]{1,0:T(8,128)} %bitcast.9, bf16[9,32,128]{2,1,0:T(8,128)(2,1)} %bitcast.7, bf16[648,512]{1,0:T(8,128)(2,1)} %cmat.1, f32[512]{0:T(512)} %coff.1, f32[512]{0:T(512)} %g1.1, bf16[9,16,21]{2,1,0:T(8,128)(2,1)} %bitcast.8, ...), custom_call_target="tpu_custom_call" | custom-call | flops 3000000000 | bytes 9000000 | tf_op jit(solution)/shard_map/pallas_call | solution.py:555
  27.0 0.7 %copy.15 = bf16[16,24,512]{2,1,0:T(8,128)(2,1)} copy(bf16[16,24,512]{2,1,0:T(8,128)(2,1)S(1)} %bitcast.5) | data formatting | bytes 786432

commit v5 on v4

--- a/solution.py
+++ b/solution.py
@@ -338,6 +338,7 @@
         lane = lax.broadcasted_iota(jnp.int32, (1, 4 * SLOT), 1)
         dev = lane // SLOT
         place = lane - dev * SLOT
+        dev = jnp.where(dev == 1, 2, jnp.where(dev == 2, 1, dev))
         front = place < FRONT
         side = place - FRONT
         cycle = jnp.where(front, place // INNER, side // 4)
@@ -373,8 +374,7 @@
                 )
 
     def circulants():
-        @pl.loop(0, quads, unroll=4)
-        def _(q):
+        for q in range(quads):
             for t in range(CAP):
                 rows = []
                 for k in range(BASIS):
@@ -392,10 +392,12 @@
                     sort[t],
                     preferred_element_type=f32,
                 )
-                lhs[
-                    t * PAD_ROWS : t * PAD_ROWS + BASIS * COLS,
-                    pl.ds(pl.multiple_of(4 * SLOT * q, 128), 4 * SLOT),
-                ] = block.astype(bf16)
+                block = block.astype(bf16)
+                at = slice(t * PAD_ROWS, t * PAD_ROWS + BASIS * COLS)
+                for odd in range(2):
+                    lhs[odd, at, 2 * SLOT * q : 2 * SLOT * (q + 1)] = block[
+                        :, 2 * SLOT * odd : 2 * SLOT * (odd + 1)
+                    ]
 
     @pl.when(jnp.logical_not(polar))
     def _():
@@ -489,16 +491,23 @@
         finish(big, 6)
         pass_on(0)
         pass_on(1)
+        lead = jnp.where(north, 0, 1)
+
+        def whole_cycles(odd):
+            rows = jnp.concatenate([gath[n] for n in range(odd, nlon, 2)], axis=0)
+            got = jnp.dot(lhs[odd], rows, preferred_element_type=f32)
+            return [got[t * PAD_ROWS : t * PAD_ROWS + BASIS * COLS] for t in range(CAP)]
+
+        pres[jnp.where(north, 3, 0)] = jnp.zeros((BASIS * COLS, FEAT), f32)
+        for t, got in enumerate(whole_cycles(0)):
+            pres[t + lead] = got
         finish(big + 6, 6)
 
         for m in range(chips):
             hand(m, 0, False).wait_recv()
             hand(m, 1, False).wait_recv()
-        got = jnp.dot(lhs[...], gath[...].reshape(span, FEAT), preferred_element_type=f32)
-        lead = jnp.where(north, 0, 1)
-        pres[jnp.where(north, 3, 0)] = jnp.zeros((BASIS * COLS, FEAT), f32)
-        for t in range(CAP):
-            pres[t + lead] = got[t * PAD_ROWS : t * PAD_ROWS + BASIS * COLS]
+        for t, got in enumerate(whole_cycles(1)):
+            pres[t + lead] += got
         filter_pair(small, 0)
         filter_pair(small + 2, 2)
         finish(small, 4)
@@ -542,7 +551,7 @@
         vmem((EXT_ROWS, EXT_COLS, FEAT), f32),
         vmem((ROWS * COLS, BASIS * FEAT), bf16),
         vmem((nlon, SLOT, FEAT), bf16),
-        vmem((CAP * PAD_ROWS, span), bf16),
+        vmem((2, CAP * PAD_ROWS, span // 2), bf16),
         vmem((4, BASIS * COLS, FEAT), f32),
         pltpu.SemaphoreType.DMA((13,)),
         pltpu.SemaphoreType.DMA((10,)),

time: 27.9 us -> 27.4 us (0.982)
  Pallas kernels: 27 us -> 26.4 us
    pallas_call x1, Pallas kernels: 27 us -> 26.4 us  [body(): pl.pallas_call(functools.partial(kernel, nlat, nlon), out_shape=pltpu.VME...]
where the time goes in v5:
time: 27.4 us; the launch traced here: 27.2 us
  Pallas kernels  26.4 us (96%)
  local copies, waits for them, and re-layouts  0.75 us (3%)
    pallas_call x1, Pallas kernels, body(): pl.pallas_call(functools.partial(kernel, nlat, nlon), out_shape=pltpu.VME...  26.4 us
    unnamed x1, local copies, waits for them, and re-layouts  0.75 us

profile of v5, /device:TPU:1, one launch (start us, length us, event | category | flops | bytes accessed | tf_op | source)
XLA Modules:
  0.0 27.2 jit_solution(1322986117359072065)
XLA Ops:
  0.0 26.4 %shard_map.127 = bf16[384,512]{1,0:T(8,128)(2,1)S(1)} custom-call(bf16[32,48,72]{2,1,0:T(8,128)(2,1)} %x.1, s32[32,128]{1,0:T(8,128)} %bitcast.9, bf16[9,32,128]{2,1,0:T(8,128)(2,1)} %bitcast.7, bf16[648,512]{1,0:T(8,128)(2,1)} %cmat.1, f32[512]{0:T(512)} %coff.1, f32[512]{0:T(512)} %g1.1, bf16[9,16,21]{2,1,0:T(8,128)(2,1)} %bitcast.8, ...), custom_call_target="tpu_custom_call" | custom-call | flops 3000000000 | bytes 9000000 | tf_op jit(solution)/shard_map/pallas_call | solution.py:564
  26.4 0.7 %copy.15 = bf16[16,24,512]{2,1,0:T(8,128)(2,1)} copy(bf16[16,24,512]{2,1,0:T(8,128)(2,1)S(1)} %bitcast.5) | data formatting | bytes 786432
